TPU v7x, 128 devices: a whole 4x4x4 slice. The times are simulated.
128 devices in a mesh: section: 2 (over core), replica: 4 (over y), shard: 16 (over x, z).
Axes of the slice: x: 4, y: 4, z: 4, core: 2. Of those that a mesh axis runs over, the one named last changes fastest.
Arguments:
- inputs: bfloat16 [2, 49152, 512], P(None, ('replica', 'shard')), may hold values from -6 to 6
- cotangent: bfloat16 [2, 49152, 512], P(None, ('replica', 'shard')), may hold values from -6 to 6
- lengths: int32 [2, 64, 4], P(None, ('replica', 'shard')), may hold values from 0 to 768, as said below
- norm1_gain: bfloat16 [2, 512], P('section', 'shard'), may hold values from 0.5 to 1.5
- norm1_bias: bfloat16 [2, 512], P('section', 'shard'), may hold values from -1.5 to 1.5
- qkv_weight: bfloat16 [2, 512, 1536], P('section', 'shard'), may hold values from -0.375 to 0.375
- qkv_bias: bfloat16 [2, 1536], P('section', 'shard'), may hold values from -2.5 to 2.5
- dense_weight: bfloat16 [2, 512, 512], P('section', 'shard'), may hold values from -1 to 1
- norm2_gain: bfloat16 [2, 512], P('section', 'shard'), may hold values from 0.5 to 1.5
- norm2_bias: bfloat16 [2, 512], P('section', 'shard'), may hold values from -1.5 to 1.5
- fc_in_weight: bfloat16 [2, 512, 2048], P('section', 'shard'), may hold values from -0.25 to 0.25
- fc_in_bias: bfloat16 [2, 2048], P('section', 'shard'), may hold values from -2.5 to 2.5
- fc_out_weight: bfloat16 [2, 2048, 512], P('section', 'shard'), may hold values from -0.1875 to 0.1875
- out_bias: bfloat16 [2, 512], P('section', 'shard'), may hold values from -2.5 to 2.5
Outputs:
- activations: bfloat16 [2, 2, 49152, 512], P('section', None, ('replica', 'shard'))
- input_grads: bfloat16 [2, 2, 49152, 512], P('section', None, ('replica', 'shard'))
- grad_norm1_gain: float32 [2, 512], P('section', 'shard')
- grad_norm1_bias: float32 [2, 512], P('section', 'shard')
- grad_qkv_weight: float32 [2, 512, 1536], P('section', 'shard')
- grad_qkv_bias: float32 [2, 1536], P('section', 'shard')
- grad_dense_weight: float32 [2, 512, 512], P('section', 'shard')
- grad_norm2_gain: float32 [2, 512], P('section', 'shard')
- grad_norm2_bias: float32 [2, 512], P('section', 'shard')
- grad_fc_in_weight: float32 [2, 512, 2048], P('section', 'shard')
- grad_fc_in_bias: float32 [2, 2048], P('section', 'shard')
- grad_fc_out_weight: float32 [2, 2048, 512], P('section', 'shard')
- grad_out_bias: float32 [2, 512], P('section', 'shard')
Inputs may be any that keep to these rules, and one draw needn't show every extreme that they name: `lengths`: in each slab the sequences, each padded up to a multiple of 128 rows, fill at most 768 rows; a length of 0 is an empty sequence. In every micro-batch some slab holds a single sequence of 768 rows.
All inputs are finite; a program needn't handle non-finite values.
Results may differ from a plain program's by a relative error of at most 0.025.
Values may be sent and summed in bfloat16 or wider, within the bound.
A program may use at most 256 MiB of HBM per device.

v0:
```python
import math

import jax
import jax.numpy as jnp
from jax import lax
from jax.experimental import pallas as pl
from jax.experimental.pallas import tpu as pltpu
from jax.sharding import PartitionSpec as P

T = 768
D = 512
FF = 2048
HEADS = 8
HEAD = 64
ROT = 16
BLOCK = 128
SEQS = 4
TILE = 256
EPS = 1e-5
MASKED = -1e9
LOG2E = 1.0 / math.log(2.0)
LN2 = math.log(2.0)
MESH = pl.DeviceIdType.MESH
BF = jnp.bfloat16
F32 = jnp.float32

PAIRS = 4
DENSE, FIN, FOUT, VEC = 4, 5, 6, 7
PARTS = 8
LETTERS = "abcdDIOV"
HALF_ROWS = (16, 16, 16, 16, 16, 16, 64, 8)
WIDTH = (384, 384, 384, 384, 512, 2048, 512, 128)
KIND = (BF, BF, BF, BF, BF, BF, BF, F32)


def dg(a, b, ca, cb):
    return lax.dot_general(a, b, (((ca,), (cb,)), ((), ())), preferred_element_type=F32)


class Place:
    def __init__(self):
        self.s = lax.axis_index("section")
        self.y = lax.axis_index("replica")
        shard = lax.axis_index("shard")
        x, z = shard // 4, shard % 4
        self.shard, self.x, self.z = shard, x, z
        self.p = x + self.s * (z - x)
        self.q = z + self.s * (x - z)

    def at(self, p, q):
        return (1 - self.s) * (4 * p + q) + self.s * (4 * q + p)

    def sibling(self):
        return (1 - self.s, self.y, self.shard)

    def along_p(self, d):
        return (self.s, self.y, self.at((self.p + d) % 4, self.q))

    def along_q(self, d):
        return (self.s, self.y, self.at(self.p, (self.q + d) % 4))

    def along_y(self, d):
        return (self.s, (self.y + d) % 4, self.shard)


def remote(src, dst, send, recv, device):
    return pltpu.make_async_remote_copy(
        src_ref=src, dst_ref=dst, send_sem=send, recv_sem=recv, device_id=device, device_id_type=MESH
    )


class Gather:
    def __init__(self, me, layer, part, shard_ref, whole, send, recv, local):
        self.me, self.layer, self.part = me, layer, part
        self.shard_ref, self.w = shard_ref, whole
        self.send = lambda k: send.at[layer, part, k]
        self.recv = lambda k: recv.at[layer, part, k]
        self.local = local.at[part]
        self.rows = HALF_ROWS[part]
        self.direct = layer == 0 and part in (0, 1, 2, 3, VEC)
        self.ways = (1, 3, 2) if self.direct else (1, 3)

    def halves(self, h, target):
        if self.part == VEC:
            return [(self.shard_ref.at[h], target)]
        rows = pl.ds(pl.multiple_of(h * self.rows, self.rows), self.rows)
        if self.part < PAIRS:
            return [
                (
                    self.shard_ref.at[0, rows, pl.ds(512 * which + 128 * self.part, 128)],
                    target.at[:, pl.ds(128 * which, 128)],
                )
                for which in range(3)
            ]
        return [(self.shard_ref.at[0, rows, :], target)]

    def move(self, ref, sent, came, device):
        return remote(ref, ref, self.send(sent), self.recv(came), device)

    def shards(self, count):
        return self.move(self.w.at[self.me.s, pl.ds(0, count)], 1, 1, self.me.sibling())

    def row(self, half, p):
        return self.w.at[half, pl.ds(4 * p, 4)]

    def own(self, half, p, q):
        return self.w.at[half, 4 * p + q]

    def step0(self):
        me = self.me

        @pl.when(me.s == self.layer)
        def _():
            for src, dst in self.halves(me.s, self.own(me.s, me.p, me.q)):
                pltpu.make_async_copy(src, dst, self.local).start()
            for src, dst in self.halves(1 - me.s, self.own(1 - me.s, me.q, me.p)):
                remote(src, dst, self.send(0), self.recv(0), me.sibling()).start()

    def step1(self):
        me = self.me
        own = self.own(me.s, me.p, me.q)

        @pl.when(me.s == self.layer)
        def _():
            pltpu.make_async_copy(own, own, self.local).wait()

        @pl.when(me.s != self.layer)
        def _():
            self.move(own, 0, 0, me.sibling()).wait_recv()

        for d in (1, 3, 2):
            self.move(own, 1, 1, me.along_q(d)).start()

    def across(self, p):
        self.move(self.row(self.me.s, p), 2, 4, self.me.sibling()).start()

    def step2(self):
        me = self.me
        self.shards(3).wait_recv()
        for d in self.ways:
            self.move(self.row(me.s, me.p), 1, 2, me.along_p(d)).start()
        self.across(me.p)

    def step3(self):
        me = self.me
        ref = self.w.at[me.s, pl.ds(0, 4 * len(self.ways))]
        self.move(ref, 1, 2, me.sibling()).wait_recv()
        if not self.direct:
            for d in (1, 3):
                half = self.w.at[me.s, pl.ds(4 * ((me.p + 4 - d) % 4) + d - 1, 2)]
                self.move(half, 1, 3, me.along_p(d)).start()
        for d in self.ways:
            self.across((me.p + 4 - d) % 4)

    def step4(self):
        me = self.me
        if not self.direct:
            self.move(self.row(me.s, me.p), 1, 3, me.sibling()).wait_recv()
            self.across((me.p + 2) % 4)

    def step5(self):
        self.move(self.w.at[1 - self.me.s], 2, 4, self.me.sibling()).wait_recv()

    def finish(self):
        me = self.me

        @pl.when(me.s == self.layer)
        def _():
            self.move(self.own(1 - me.s, me.q, me.p), 0, 0, me.sibling()).wait_send()

        self.shards(15).wait_send()
        self.move(self.w.at[me.s], 2, 4, me.sibling()).wait_send()


class Reduce:
    def __init__(self, me, layer, part, terms, buffers, send, recv):
        self.me, self.layer, self.part = me, layer, part
        self.g = terms
        self.r, self.one, self.two, self.ys, self.f, self.out = buffers
        self.send = lambda k: send.at[layer, part, k]
        self.recv = lambda k: recv.at[layer, part, k]
        self.kind = KIND[part]

    def swap(self):
        me = self.me
        return remote(self.g.at[1 - me.s], self.r, self.send(0), self.recv(0), me.sibling())

    def first(self, d):
        me = self.me
        row = self.r.at[pl.ds(4 * ((me.p + d) % 4), 4)]
        return remote(row, self.one.at[d - 1], self.send(1), self.recv(1), me.along_p(d))

    def second(self, d):
        me = self.me
        shard = self.r.at[4 * me.p + (me.q + d) % 4]
        return remote(shard, self.two.at[d - 1], self.send(2), self.recv(2), me.along_q(d))

    def third(self, d):
        me = self.me
        return remote(self.ys.at[me.y], self.ys.at[me.y], self.send(3), self.recv(3), me.along_y(d))

    def all_of(self, ref, k):
        return remote(ref, ref, self.send(k), self.recv(k), self.me.sibling())

    def back(self):
        me = self.me
        return remote(self.f, self.out.at[me.s], self.send(4), self.recv(4), me.sibling())

    def step0(self):
        self.swap().start()

    def step1(self):
        me = self.me
        self.swap().wait_recv()

        def one(k, c):
            self.r[k] = (self.r[k].astype(F32) + self.g[me.s, k].astype(F32)).astype(self.kind)
            return c

        lax.fori_loop(0, 16, one, 0)
        for d in (1, 3, 2):
            self.first(d).start()
        self.swap().wait_send()

    def step2(self):
        me = self.me
        self.all_of(self.one, 1).wait_recv()

        def one(b, c):
            total = self.r[4 * me.p + b].astype(F32) + self.one[0, b].astype(F32)
            total = total + (self.one[1, b].astype(F32) + self.one[2, b].astype(F32))
            self.r[4 * me.p + b] = total.astype(self.kind)
            return c

        lax.fori_loop(0, 4, one, 0)
        for d in (1, 3, 2):
            self.second(d).start()

    def step3(self):
        me = self.me
        self.all_of(self.two, 2).wait_recv()
        total = self.r[4 * me.p + me.q].astype(F32) + self.two[0].astype(F32)
        total = total + (self.two[1].astype(F32) + self.two[2].astype(F32))
        self.ys[me.y] = total.astype(self.kind)
        for d in (1, 3, 2):
            self.third(d).start()

    def step4(self):
        me = self.me
        self.all_of(self.ys.at[pl.ds(0, 3)], 3).wait_recv()
        total = (self.ys[0].astype(F32) + self.ys[1].astype(F32)) + (
            self.ys[2].astype(F32) + self.ys[3].astype(F32)
        )

        @pl.when(me.s == self.layer)
        def _():
            self.out[me.s] = total

        @pl.when(me.s != self.layer)
        def _():
            self.f[...] = total
            self.back().start()

    def step5(self):
        me = self.me

        @pl.when(me.s == self.layer)
        def _():
            self.all_of(self.out.at[1 - me.s], 4).wait_recv()

    def finish(self):
        self.all_of(self.one, 1).wait_send()
        self.all_of(self.two, 2).wait_send()
        self.all_of(self.ys.at[pl.ds(0, 3)], 3).wait_send()

        @pl.when(self.me.s != self.layer)
        def _():
            self.back().wait_send()


class ReduceVectors:
    def __init__(self, me, layer, terms, buffers, send, recv):
        self.me, self.layer, self.g = me, layer, terms
        self.r, self.one, self.ys, self.out = buffers
        self.send = lambda k: send.at[layer, VEC, k]
        self.recv = lambda k: recv.at[layer, VEC, k]

    def swap(self):
        return remote(self.g, self.r, self.send(0), self.recv(0), self.me.sibling())

    def first(self, k):
        x, z = (self.me.x + k // 4) % 4, (self.me.z + k % 4) % 4
        device = (self.me.s, self.me.y, 4 * x + z)
        return remote(self.r.at[x, z], self.one.at[k], self.send(1), self.recv(1), device)

    def all_first(self):
        ref = self.one.at[pl.ds(1, 15)]
        return remote(ref, ref, self.send(1), self.recv(1), self.me.sibling())

    def third(self, d):
        me = self.me
        return remote(self.ys.at[me.y], self.ys.at[me.y], self.send(3), self.recv(3), me.along_y(d))

    def all_third(self):
        ref = self.ys.at[pl.ds(0, 3)]
        return remote(ref, ref, self.send(3), self.recv(3), self.me.sibling())

    def owner(self, step):
        pl.when(self.me.s == self.layer)(step)

    def step0(self):
        @pl.when(self.me.s != self.layer)
        def _():
            self.swap().start()

    def step1(self):
        def step():
            self.swap().wait_recv()
            self.r[...] += self.g[...]
            for k in (1, 4, 3, 12, 5, 7, 13, 15, 2, 8, 6, 9, 11, 14, 10):
                self.first(k).start()

        self.owner(step)

        @pl.when(self.me.s != self.layer)
        def _():
            self.swap().wait_send()

    def step2(self):
        def step():
            self.all_first().wait_recv()
            total = self.r[self.me.x, self.me.z]
            for k in range(1, 16):
                total = total + self.one[k]
            self.ys[self.me.y] = total
            for d in (1, 3, 2):
                self.third(d).start()

        self.owner(step)

    def step3(self):
        def step():
            self.all_third().wait_recv()
            self.out[...] = (self.ys[0] + self.ys[1]) + (self.ys[2] + self.ys[3])

        self.owner(step)

    def step5(self):
        pass

    def finish(self):
        def step():
            self.all_first().wait_send()
            self.all_third().wait_send()

        self.owner(step)


def natural_rows(ref, columns):
    pieces = []
    for x in range(4):
        for z in range(4):
            pieces.append(ref[0, 4 * x + z, :, columns])
            pieces.append(ref[1, 4 * z + x, :, columns])
    return jnp.concatenate(pieces, axis=0)


def group_rows(ref, x):
    pieces = []
    for z in range(4):
        pieces.append(ref[0, 4 * x + z])
        pieces.append(ref[1, 4 * z + x])
    return jnp.concatenate(pieces, axis=0)


def put_natural(ref, columns, value):
    for x in range(4):
        for z in range(4):
            row = 32 * (4 * x + z)
            ref[0, 4 * x + z, :, columns] = value[row : row + 16]
            ref[1, 4 * z + x, :, columns] = value[row + 16 : row + 32]


def put_group(ref, x, value, rows):
    for z in range(4):
        row = 2 * rows * z
        ref[0, 4 * x + z] = value[row : row + rows]
        ref[1, 4 * z + x] = value[row + rows : row + 2 * rows]


def to_column(row):
    here = lax.broadcasted_iota(jnp.int32, (128, 128), 0) == lax.broadcasted_iota(
        jnp.int32, (128, 128), 1
    )
    return jnp.sum(jnp.where(here, row, 0.0), axis=1, keepdims=True)


def turn(rows, cosine, sine):
    pieces = []
    for e in (0, 64):
        low, high = rows[e : e + 8], rows[e + 8 : e + 16]
        pieces += [low * cosine - high * sine, high * cosine + low * sine, rows[e + 16 : e + 64]]
    return jnp.concatenate(pieces, axis=0)


def columns(start, size):
    return pl.ds(pl.multiple_of(start, size), size)


def loop(count, step):
    def one(k, c):
        step(k)
        return c

    lax.fori_loop(0, count, one, 0)


def kernel(
    lengths,
    x_ref,
    cot_ref,
    wq_ref,
    wd_ref,
    wi_ref,
    wo_ref,
    gain1_ref,
    shift1_ref,
    gain2_ref,
    shift2_ref,
    last_ref,
    qkvb_ref,
    finb_ref,
    act_out,
    ig_out,
    gq_out,
    gd_out,
    gi_out,
    go_out,
    gv_out,
    st_qkv,
    st_p0,
    st_p1,
    st_p2,
    st_bt,
    st_rinv,
    st_act,
    st_slo,
    *scratch,
):
    scratch = list(scratch)

    def take(count):
        taken, scratch[:count] = scratch[:count], []
        return taken

    def take_parts(count=4):
        pairs, *rest = take(count)
        return [pairs] + [pairs.at[k] for k in range(PAIRS)] + rest

    (wq0, *w0), (wq1, *w1) = take_parts(5), take_parts(5)
    w, wq = (w0, w1), (wq0, wq1)
    gq, *g = take_parts()
    r, one, two, ys = [(take_parts(), take_parts()) for _ in range(4)]
    rq = [parts.pop(0) for parts in r]
    for both in (one, two, ys):
        for parts in both:
            parts.pop(0)
    f = take_parts()[1:]
    gvec, *rvec = take(3)
    vecs, yvec, (vsrc, vrow) = take(2), take(2), take(2)
    hid, grad, n1t, n2, acc, carried = take(6)
    qkvt, p0, p1, p2, bt, rinv, act, slo = take(8)
    d0, d1, d2, scores_one = take(4)
    dn1 = n2
    vd, vq, vf, dvec, fvec, live, bias, cos_ref, sin_ref = take(9)
    sends, ag_recv, rs_recv, ag_local, sems, ex_send, ex_recv = take(7)
    probs = (p0, p1, p2)
    dscores = (d0, d1, d2)
    outs = [gq_out.at[k] for k in range(PAIRS)] + [gd_out, gi_out, go_out]
    shards = [wq_ref] * PAIRS + [wd_ref, wi_ref, wo_ref, vsrc]

    me = Place()
    s = me.s
    barrier = pltpu.get_barrier_semaphore()
    partners = [me.sibling()]
    for d in (1, 2, 3):
        partners += [me.along_q(d), me.along_p(d), me.along_y(d)]
        for e in (1, 2, 3):
            partners.append((s, me.y, 4 * ((me.x + d) % 4) + (me.z + e) % 4))
    for device in partners:
        pl.semaphore_signal(barrier, inc=1, device_id=device, device_id_type=MESH)
    pl.semaphore_wait(barrier, len(partners))

    gather = [
        [Gather(me, l, c, shards[c], w[l][c], sends, ag_recv, ag_local) for c in range(PARTS)]
        for l in (0, 1)
    ]
    reduce = [
        [
            Reduce(
                me, l, c, g[c], (r[l][c], one[l][c], two[l][c], ys[l][c], f[c], outs[c]), sends, rs_recv
            )
            for c in range(VEC)
        ]
        + [ReduceVectors(me, l, gvec, (rvec[l], vecs[l], yvec[l], gv_out), sends, rs_recv)]
        for l in (0, 1)
    ]

    def fetch(*plan):
        for word in plan:
            item = gather[int(word[0])][LETTERS.index(word[1])]
            getattr(item, "step" + word[2])()

    def back_pairs(l, first):
        def step(k):
            hp = first + k
            back_attend(l, hp)
            back_qkv(hp)
            remote(
                gq.at[hp, 1 - s], rq[l].at[hp], sends.at[l, hp, 0], rs_recv.at[l, hp, 0], me.sibling()
            ).start()

        loop(2, step)

    def send(*plan):
        for word in plan:
            item = reduce[int(word[0])][LETTERS.index(word[1])]
            getattr(item, "step" + word[2])()

    vsrc[...] = jnp.zeros((2, 8, 128), F32)
    for k in range(4):
        here = me.z == k
        for row, ref in enumerate((gain1_ref, shift1_ref, gain2_ref, shift2_ref, last_ref)):
            vsrc[0, row : row + 1, 32 * k : 32 * k + 32] = jnp.where(here, ref[...].astype(F32), 0.0)
        vrow[0:1, 96 * k : 96 * k + 96] = jnp.where(here, qkvb_ref[...].astype(F32), 0.0)
    for k in range(3):
        vsrc[1, k : k + 1, :] = vrow[0:1, 128 * k : 128 * k + 128]
    vsrc[1, 3:4, :] = finb_ref[...].astype(F32)

    x_in = pltpu.make_async_copy(x_ref.at[s], hid.at[0], sems.at[0])
    cot_in = pltpu.make_async_copy(cot_ref.at[s], grad.at[0], sems.at[1])
    x_in.start()
    fetch("0V0", "0a0", "0b0", "0c0", "0d0", "0I0", "0D0", "0O0", "1V0", "1a0", "1b0", "1c0", "1d0", "1I0", "1D0", "1O0")
    fetch("0V1", "0a1", "0b1", "0c1", "0d1", "0D1", "0I1", "0O1")
    cot_in.start()

    starts, ends, at = [], [], jnp.int32(0)
    for k in range(SEQS):
        size = lengths[s, 0, k]
        starts.append(at)
        ends.append(at + size)
        at = at + (size + BLOCK - 1) // BLOCK * BLOCK

    def inside(places):
        return [(places >= a) & (places < b) for a, b in zip(starts, ends)]

    def live_tile(k):
        places = lax.broadcasted_iota(jnp.int32, (TILE, 1), 0) + k * TILE
        total = jnp.zeros((TILE, 1), F32)
        for found in inside(places):
            total = total + jnp.where(found, 1.0, 0.0)
        live[columns(k * TILE, TILE), :] = total

    loop(3, live_tile)
    places = lax.broadcasted_iota(jnp.int32, (8, T), 1)
    begin = jnp.zeros((8, T), jnp.int32)
    offset = jnp.zeros((8, T), jnp.int32)
    for found, a in zip(inside(places), starts):
        begin = begin + jnp.where(found, a, 0)
        offset = offset + jnp.where(found, places - a, 0)
    rates = jnp.exp(
        lax.broadcasted_iota(jnp.int32, (8, T), 0).astype(F32) * (-2.0 * math.log(10000.0) / ROT)
    )
    angles = offset.astype(F32) * rates
    cos_ref[...] = jnp.cos(angles)
    sin_ref[...] = jnp.sin(angles)
    for j in range(3):
        for i in range(j + 1):
            keys = lax.broadcasted_iota(jnp.int32, (TILE, TILE), 0) + i * TILE
            queries = lax.broadcasted_iota(jnp.int32, (TILE, TILE), 1) + j * TILE
            fits = (keys >= begin[0:1, j * TILE : (j + 1) * TILE]) & (keys <= queries)
            bias[j * (j + 1) // 2 + i] = jnp.where(fits, 0.0, MASKED)

    def unpack(l):
        ref = w[l][VEC]
        for x in range(4):
            vd[:, 128 * x : 128 * x + 128] = (ref[0, 4 * x] + ref[0, 4 * x + 1]) + (
                ref[0, 4 * x + 2] + ref[0, 4 * x + 3]
            )
            group = (ref[1, x] + ref[1, 4 + x]) + (ref[1, 8 + x] + ref[1, 12 + x])
            for k in range(3):
                vq[3 * x + k : 3 * x + k + 1, :] = group[k : k + 1]
            for z in range(4):
                vf[x : x + 1, 128 * z : 128 * z + 128] = ref[1, 4 * z + x][3:4]

    def normed(l, rows):
        v = hid[l, rows, :].astype(F32)
        centred = v - jnp.mean(v, axis=1, keepdims=True)
        scale = lax.rsqrt(jnp.mean(centred * centred, axis=1, keepdims=True) + EPS)
        return centred * scale, scale

    def norms(l):
        def tile(k):
            rows = columns(k * TILE, TILE)
            u, _ = normed(l, rows)
            n1t[:, rows] = (u * vd[0:1, :] + vd[1:2, :]).astype(BF).T
            n2[rows, :] = (u * vd[2:3, :] + vd[3:4, :]).astype(BF)

        loop(3, tile)

    def project(l, hp):
        value = dg(natural_rows(wq[l].at[hp], slice(0, 384)), n1t[...], 0, 0)
        pair = []
        for which in range(3):
            part = value[128 * which : 128 * which + 128] + to_column(vq[pl.ds(which * 4 + hp, 1), :])
            if which < 2:
                part = turn(part, cos_ref[...], sin_ref[...])
            if which == 0:
                part = part * (LOG2E / 8.0)
            pair.append(part.astype(BF))
            qkvt[columns(hp * 384 + which * 128, 128), :] = pair[which]
        return pair

    def score_block(e, k):
        if e:
            return scores_one.at[k]
        return acc.at[pl.ds(TILE * (k // 2), TILE), pl.ds(TILE * (k % 2), TILE)]

    def attend(l, hp):
        pair = project(l, hp)
        keys = pair[1].T
        blank = jnp.zeros((HEAD, T), BF)
        peaks = ([None] * 3, [None] * 3)
        for e in (0, 1):
            mine = pair[0][e * HEAD : (e + 1) * HEAD]
            mine = jnp.concatenate([mine, blank] if e == 0 else [blank, mine], axis=0)
            for i in range(3):
                for j in range(i, 3):
                    k = j * (j + 1) // 2 + i
                    scores = dg(keys[i * TILE : (i + 1) * TILE], mine[:, j * TILE : (j + 1) * TILE], 1, 0)
                    scores = scores + bias[k]
                    score_block(e, k)[...] = scores
                    peak = jnp.max(scores, axis=0, keepdims=True)
                    peaks[e][j] = peak if i == 0 else jnp.maximum(peaks[e][j], peak)
        for e in (0, 1):
            h = 2 * hp + e
            value = jnp.concatenate([pair[2][e * HEAD : (e + 1) * HEAD], jnp.ones((8, T), BF)], axis=0)
            for j in range(3):
                at_j = slice(j * TILE, (j + 1) * TILE)
                blended = jnp.zeros((HEAD + 8, TILE), F32)
                for i in range(j + 1):
                    raised = jnp.exp2(score_block(e, j * (j + 1) // 2 + i)[...] - peaks[e][j]).astype(BF)
                    probs[i][h, :, (j - i) * TILE : (j - i + 1) * TILE] = raised
                    blended = blended + dg(value[:, i * TILE : (i + 1) * TILE], raised, 1, 0)
                inverse = 1.0 / blended[HEAD : HEAD + 1]
                rinv[pl.ds(h, 1), at_j] = inverse
                bt[columns(hp * 128 + e * HEAD, HEAD), at_j] = (blended[:HEAD] * inverse).astype(BF)

    def widen(l, c):
        cols = columns(c * 512, 512)
        weight = natural_rows(w[l][FIN], cols)
        shift = vf[pl.ds(c, 1), :]

        def tile(k):
            rows = columns(k * TILE, TILE)
            v = dg(n2[rows, :], weight, 1, 0) + shift
            below = 0.5 + 0.5 * lax.erf(v * (1.0 / math.sqrt(2.0)))
            act[rows, cols] = (v * below).astype(BF)
            slope = below + v * (jnp.exp(-0.5 * v * v) * (1.0 / math.sqrt(2.0 * math.pi)))
            slo[rows, cols] = slope.astype(BF)

        for k in range(3):
            tile(k)

    def join(l):
        def part(t):
            cols = columns(t * TILE, TILE)
            weight = jnp.concatenate(
                [
                    piece
                    for x in range(4)
                    for z in range(4)
                    for piece in (w[l][FOUT][0, 4 * x + z, :, cols], w[l][FOUT][1, 4 * z + x, :, cols])
                ],
                axis=0,
            )
            total = dg(act[...], weight, 1, 0)
            total = total + dg(bt[...], natural_rows(w[l][DENSE], cols), 0, 0)
            total = total + hid[l, :, cols].astype(F32) + vd[4:5, cols]
            hid[l + 1, :, cols] = (total * live[...]).astype(BF)

        loop(2, part)

    def local(src, dst, k):
        return pltpu.make_async_copy(src, dst, sems.at[k])

    attention_kept = [
        (qkvt, st_qkv, 2),
        (p0, st_p0, 3),
        (p1, st_p1, 4),
        (p2, st_p2, 5),
        (bt, st_bt, 6),
        (rinv, st_rinv, 7),
    ]
    wide_kept = [(act, st_act, 8), (slo, st_slo, 9)]

    fetch("0V2", "0a2", "0b2", "0c2", "0d2")
    x_in.wait()
    fetch("0V3", "0a3")
    fetch("0D2", "0I2")
    fetch("0V5")
    unpack(0)
    norms(0)
    fetch("0b3", "0O2", "0a5")
    fetch("0c3", "0b5")
    loop(2, lambda hp: attend(0, hp))
    fetch("0d3", "0c5")
    fetch("0D3", "0I3")
    fetch("1V1", "1a1", "1b1", "1c1", "1d1", "0d5")
    loop(2, lambda hp: attend(0, hp + 2))
    for a, b, k in attention_kept:
        local(a, b, k).start()
    fetch("0O3")
    fetch("1I1", "1D1", "1O1")
    fetch("0D4", "0I4", "1V2", "1a2", "1b2")
    fetch("0I5")
    loop(2, lambda c: widen(0, c))
    fetch("0O4")
    fetch("1c2", "1d2", "1V3", "1a3")
    loop(2, lambda c: widen(0, c + 2))
    fetch("1b3", "1c3", "1d3", "1I2", "1D2", "1O2", "0D5", "0O5")
    join(0)
    for a, b, k in wide_kept:
        local(a, b, k).start()

    fetch("1V4", "1a4", "1b4")
    fetch("1V5")
    unpack(1)
    norms(1)
    fetch("1c4", "1d4", "1a5", "1b5")
    for a, b, k in attention_kept:
        local(a, b, k).wait()
    loop(2, lambda hp: attend(1, hp))
    fetch("1I3", "1D3", "1c5", "1d5")
    loop(2, lambda hp: attend(1, hp + 2))
    fetch("1O3", "1I4", "1D4")
    fetch("1I5")
    for a, b, k in wide_kept:
        local(a, b, k).wait()
    loop(2, lambda c: widen(1, c))
    fetch("1O4")
    loop(2, lambda c: widen(1, c + 2))
    fetch("1D5", "1O5")
    join(1)
    for l in (0, 1):
        for c in range(PARTS):
            gather[l][c].finish()
    act_mine = local(hid.at[1 + s], act_out.at[s], 10)
    act_theirs = remote(hid.at[2 - s], act_out.at[s], ex_send.at[0], ex_recv.at[0], me.sibling())
    act_mine.start()
    act_theirs.start()
    cot_in.wait()

    def start_back(l):
        def tile(k):
            rows = columns(k * TILE, TILE)
            v = grad[1 - l, rows, :].astype(F32) * live[rows, :]
            carried[rows, :] = v.astype(BF)
            here = jnp.sum(v, axis=0, keepdims=True)
            dvec[4:5, :] = here + jnp.where(k == 0, 0.0, dvec[4:5, :])

        dvec[...] = jnp.zeros((8, D), F32)
        loop(3, tile)

    def back_out(c):
        cols = columns(c * 512, 512)
        put_group(g[FOUT], c, dg(act[:, cols], carried[...], 0, 0).astype(BF), 64)

    def back_wide(l, c):
        cols = columns(c * 512, 512)
        weight = group_rows(w[l][FOUT], c)
        total = jnp.zeros((1, 512), F32)
        for k in range(3):
            rows = slice(k * TILE, (k + 1) * TILE)
            v = dg(carried[rows, :], weight, 1, 1) * slo[rows, cols].astype(F32)
            v = v.astype(BF)
            slo[rows, cols] = v
            total = total + jnp.sum(v.astype(F32), axis=0, keepdims=True)
        fvec[pl.ds(c, 1), :] = total

    def back_in(l, c):
        cols = columns(c * 512, 512)
        put_natural(g[FIN], cols, dg(n2[...], slo[:, cols], 0, 0).astype(BF))

    def back_norm_two(l, t):
        low = w[l][FIN][0, pl.ds(8 * t, 8)]
        high = [w[l][FIN][1, pl.ds(4 * z + 2 * t, 2)] for z in range(4)]
        pieces = []
        for x in range(2):
            for z in range(4):
                pieces += [low[4 * x + z], high[z][x]]
        acc[:, columns(t * TILE, TILE)] = dg(slo[...], jnp.concatenate(pieces, axis=0), 1, 1)

    def back_dense(l):
        put_natural(g[DENSE], slice(0, 512), dg(bt[...], carried[...], 1, 0).astype(BF))

    def back_attend(l, hp):
        weight = group_rows(w[l][DENSE], hp)
        below = dg(weight, carried[...], 1, 1)
        queries = qkvt[columns(hp * 384, 128), :]
        keys = qkvt[columns(hp * 384 + 128, 128), :]
        values = qkvt[columns(hp * 384 + 256, 128), :].T
        blended = bt[columns(hp * 128, 128), :].astype(F32)
        blank = jnp.zeros((HEAD, TILE), BF)
        downs = []
        for e in (0, 1):
            h = 2 * hp + e
            down = below[e * HEAD : (e + 1) * HEAD] * rinv[pl.ds(h, 1), :]
            centre = jnp.sum(down * blended[e * HEAD : (e + 1) * HEAD], axis=0, keepdims=True)
            down = down.astype(BF)
            downs.append(down)
            for j in range(3):
                at_j = slice(j * TILE, (j + 1) * TILE)
                mine = down[:, at_j]
                mine = jnp.concatenate([mine, blank] if e == 0 else [blank, mine], axis=0)
                for i in range(j + 1):
                    cols = slice((j - i) * TILE, (j - i + 1) * TILE)
                    slope = dg(values[i * TILE : (i + 1) * TILE], mine, 1, 0) - centre[:, at_j]
                    slope = slope * probs[i][h, :, cols].astype(F32)
                    dscores[i][e, :, cols] = slope.astype(BF)
        done = []
        for e in (0, 1):
            h = 2 * hp + e
            query = queries[e * HEAD : (e + 1) * HEAD]
            key = keys[e * HEAD : (e + 1) * HEAD]
            grad_query, grad_key, grad_value = [], [], []
            for j in range(3):
                total = jnp.zeros((HEAD, TILE), F32)
                for i in range(j + 1):
                    cols = slice((j - i) * TILE, (j - i + 1) * TILE)
                    total = total + dg(key[:, i * TILE : (i + 1) * TILE], dscores[i][e, :, cols], 1, 0)
                grad_query.append(total * 0.125)
            for i in range(3):
                grad_key.append(dg(query[:, i * TILE :], dscores[i][e], 1, 1) * LN2)
                grad_value.append(dg(downs[e][:, i * TILE :], probs[i][h], 1, 1))
            done.append(
                [jnp.concatenate(pieces, axis=1) for pieces in (grad_query, grad_key, grad_value)]
            )
        for which in range(3):
            value = jnp.concatenate([done[0][which], done[1][which]], axis=0)
            if which < 2:
                value = turn(value, cos_ref[...], -sin_ref[...])
            qkvt[columns(hp * 384 + which * 128, 128), :] = value.astype(BF)

    def back_qkv(hp):
        value = dg(n1t[...], qkvt[columns(hp * 384, 384), :], 1, 1)
        put_natural(gq.at[hp], slice(0, 384), value.astype(BF))

    def back_norm_one(l, t):
        weight = jnp.concatenate([group_rows(wq[l].at[hp], t) for hp in range(PAIRS)], axis=1)
        dn1[:, columns(t * 128, 128)] = dg(weight, qkvt[...], 1, 0).astype(BF).T

    def norm_sums(l):
        def tile(k):
            rows = columns(k * TILE, TILE)
            u, _ = normed(l, rows)
            first = dn1[rows, :].astype(F32)
            second = acc[rows, :]
            dvec[0:1, :] += jnp.sum(first * u, axis=0, keepdims=True)
            dvec[1:2, :] += jnp.sum(first, axis=0, keepdims=True)
            dvec[2:3, :] += jnp.sum(second * u, axis=0, keepdims=True)
            dvec[3:4, :] += jnp.sum(second, axis=0, keepdims=True)

        loop(3, tile)

    def end_back(l):
        def tile(k):
            rows = columns(k * TILE, TILE)
            u, scale = normed(l, rows)
            first = dn1[rows, :].astype(F32)
            second = acc[rows, :]
            total = first * vd[0:1, :] + second * vd[2:3, :]
            centre = jnp.mean(total, axis=1, keepdims=True)
            along = jnp.mean(total * u, axis=1, keepdims=True)
            total = carried[rows, :].astype(F32) + scale * (total - centre - u * along)
            grad[l, rows, :] = total.astype(BF)

        loop(3, tile)

    def put_vectors(l):
        sums = dg(jnp.ones((8, T), BF), qkvt[...], 1, 1)
        for x in range(4):
            for k in range(3):
                which, hp = divmod(3 * x + k, PAIRS)
                row = 384 * hp + 128 * which
                vq[3 * x + k : 3 * x + k + 1, :] = sums[0:1, row : row + 128]
        for x in range(4):
            rest = jnp.concatenate([vq[3 * x : 3 * x + 3, :], jnp.zeros((5, 128), F32)], axis=0)
            for z in range(4):
                gvec[x, z, 0:8] = dvec[:, 128 * x : 128 * x + 128]
                gvec[x, z, 8:16] = rest
                gvec[x, z, 11:12] = fvec[x : x + 1, 128 * z : 128 * z + 128]

    restored = ((qkvt, st_qkv, 2), (p0, st_p0, 3), (p1, st_p1, 4), (p2, st_p2, 5), (bt, st_bt, 6), (rinv, st_rinv, 7))

    start_back(1)
    loop(4, back_out)
    send("1O0")
    loop(4, lambda c: back_wide(1, c))
    send("1O1")
    loop(4, lambda c: back_in(1, c))
    send("1I0")
    loop(2, lambda t: back_norm_two(1, t))
    local(st_act, act, 8).start()
    local(st_slo, slo, 9).start()
    back_dense(1)
    send("1D0", "1I1")
    back_pairs(1, 0)
    send("1D1", "1a1", "1O2")
    back_pairs(1, 2)
    send("1b1", "1c1", "1I2")
    loop(4, lambda t: back_norm_one(1, t))
    send("1d1", "1D2", "1O3")
    norm_sums(1)
    put_vectors(1)
    for a, b, k in restored:
        local(b, a, k).start()
    send("1V0", "1a2")
    end_back(1)

    unpack(0)
    norms(0)
    start_back(0)
    local(st_act, act, 8).wait()
    local(st_slo, slo, 9).wait()
    send("1b2", "1I3")
    loop(4, back_out)
    send("0O0", "1V1", "1D3", "1c2", "1d2", "1a3")
    loop(4, lambda c: back_wide(0, c))
    send("0O1", "1O4", "1b3")
    loop(4, lambda c: back_in(0, c))
    send("0I0", "1V2", "1c3", "1d3", "1D4")
    loop(2, lambda t: back_norm_two(0, t))
    send("0I1", "1I4", "1a4", "1b4")
    for a, b, k in restored:
        local(b, a, k).wait()
    back_dense(0)
    send("0D0")
    back_attend(0, 0)
    back_qkv(0)
    send("0a0", "0D1", "1V3", "1c4", "1d4")
    back_attend(0, 1)
    back_qkv(1)
    send("0b0", "0a1", "0O2")
    back_attend(0, 2)
    back_qkv(2)
    send("0c0", "0b1")
    back_attend(0, 3)
    back_qkv(3)
    send("0d0", "0c1")
    send("0I2", "0D2", "0a2", "0O3")
    loop(2, lambda t: back_norm_one(0, t))
    send("0d1", "0b2")
    loop(2, lambda t: back_norm_one(0, t + 2))
    norm_sums(0)
    put_vectors(0)
    send("0V0")
    send("0I3", "0c2", "0D3", "0a3", "0O4")
    send("0d2")
    send("0V1")
    end_back(0)
    grad_mine = local(grad.at[s], ig_out.at[s], 11)
    grad_theirs = remote(grad.at[1 - s], ig_out.at[s], ex_send.at[1], ex_recv.at[1], me.sibling())
    grad_mine.start()
    grad_theirs.start()
    send("0b3", "0c3", "0d3")
    send("0D4", "0a4")
    send("0V2")
    send("0b4", "0c4")
    send("0d4")
    send("0I4")
    send("0V3")
    for l in (1, 0):
        for c in range(PARTS):
            reduce[l][c].step5()
            reduce[l][c].finish()
    act_mine.wait()
    act_theirs.wait_send()
    remote(hid.at[2 - s], act_out.at[1 - s], ex_send.at[0], ex_recv.at[0], me.sibling()).wait_recv()
    grad_mine.wait()
    grad_theirs.wait_send()
    remote(grad.at[1 - s], ig_out.at[1 - s], ex_send.at[1], ex_recv.at[1], me.sibling()).wait_recv()


def scratch_shapes():
    def parts(lead, kind=None):
        return [pltpu.VMEM((PAIRS, *lead, HALF_ROWS[0], WIDTH[0]), kind or BF)] + [
            pltpu.VMEM((*lead, HALF_ROWS[c], WIDTH[c]), kind or KIND[c]) for c in range(PAIRS, PARTS)
        ]

    shapes = []
    for _ in (0, 1):
        shapes += parts((2, 16))
    for lead in ((2, 16), (16,), (16,), (3, 4), (3, 4), (3,), (3,), (4,), (4,)):
        shapes += parts(lead)[:-1]
    shapes += parts((), F32)[:-1]
    for lead in ((4, 4), (4, 4), (4, 4), (16,), (16,), (4,), (4,)):
        shapes.append(pltpu.VMEM((*lead, 16, 128), F32))
    shapes += [pltpu.VMEM((2, 8, 128), F32), pltpu.VMEM((8, 384), F32)]
    shapes += [
        pltpu.VMEM((3, T, D), BF),
        pltpu.VMEM((2, T, D), BF),
        pltpu.VMEM((D, T), BF),
        pltpu.VMEM((T, D), BF),
        pltpu.VMEM((T, D), F32),
        pltpu.VMEM((T, D), BF),
    ]
    shapes += [pltpu.VMEM(shape, kind) for shape, kind in KEPT]
    shapes += [
        pltpu.VMEM((2, TILE, 768), BF),
        pltpu.VMEM((2, TILE, 512), BF),
        pltpu.VMEM((2, TILE, 256), BF),
        pltpu.VMEM((6, TILE, TILE), F32),
    ]
    shapes += [
        pltpu.VMEM((8, D), F32),
        pltpu.VMEM((16, 128), F32),
        pltpu.VMEM((8, 512), F32),
        pltpu.VMEM((8, D), F32),
        pltpu.VMEM((8, 512), F32),
        pltpu.VMEM((T, 1), F32),
        pltpu.VMEM((6, TILE, TILE), F32),
        pltpu.VMEM((8, T), F32),
        pltpu.VMEM((8, T), F32),
    ]
    dma = pltpu.SemaphoreType.DMA
    shapes += [dma((2, PARTS, 5))] * 3
    shapes += [dma((PARTS,)), dma((12,)), dma((2,)), dma((2,))]
    return shapes


KEPT = (
    ((3 * D, T), BF),
    ((HEADS, TILE, 768), BF),
    ((HEADS, TILE, 512), BF),
    ((HEADS, TILE, 256), BF),
    ((D, T), BF),
    ((HEADS, T), F32),
    ((T, FF), BF),
    ((T, FF), BF),
)


def body(
    inputs,
    cotangent,
    lengths,
    norm1_gain,
    norm1_bias,
    qkv_weight,
    qkv_bias,
    dense_weight,
    norm2_gain,
    norm2_bias,
    fc_in_weight,
    fc_in_bias,
    fc_out_weight,
    out_bias,
):
    hbm = pl.BlockSpec(memory_space=pl.ANY)
    vmem = pl.BlockSpec(memory_space=pltpu.VMEM)
    shape = jax.ShapeDtypeStruct
    results = pl.pallas_call(
        kernel,
        out_shape=[shape((2, T, D), BF), shape((2, T, D), BF), shape((PAIRS, 2, 16, 384), F32)]
        + [shape((2, HALF_ROWS[c], WIDTH[c]), F32) for c in range(PAIRS, VEC)]
        + [shape((16, 128), F32)]
        + [shape(s, k) for s, k in KEPT],
        in_specs=[pl.BlockSpec(memory_space=pltpu.SMEM)] + [hbm] * 6 + [vmem] * 7,
        out_specs=[hbm] * 2 + [vmem] * 5 + [hbm] * len(KEPT),
        scratch_shapes=scratch_shapes(),
        compiler_params=pltpu.CompilerParams(
            collective_id=0, has_side_effects=True, vmem_limit_bytes=64 * 1024 * 1024
        ),
        name="layers",
    )(
        lengths,
        inputs,
        cotangent,
        qkv_weight,
        dense_weight,
        fc_in_weight,
        fc_out_weight,
        norm1_gain,
        norm1_bias,
        norm2_gain,
        norm2_bias,
        out_bias,
        qkv_bias,
        fc_in_bias,
    )
    vector, slab = shape((1, 32), F32), shape((1, 2, T, D), BF)
    return pl.pallas_call(
        hand_out,
        out_shape=[slab, slab, vector, vector, shape((1, 32, 1536), F32), shape((1, 96), F32)]
        + [shape((1, 32, 512), F32), vector, vector, shape((1, 32, 2048), F32), shape((1, 128), F32)]
        + [shape((1, 128, 512), F32), vector],
        in_specs=[hbm] * 7,
        out_specs=[hbm] * 2 + [vmem] * 11,
        scratch_shapes=[pltpu.VMEM((4, T, D), BF)]
        + [pltpu.VMEM(r.shape, r.dtype) for r in results[2:7]]
        + [pltpu.SemaphoreType.DMA((9,)), pltpu.SemaphoreType.DMA((4,))],
        compiler_params=pltpu.CompilerParams(vmem_limit_bytes=60 * 1024 * 1024),
        name="hand_out",
    )(*results[:7])


def hand_out(
    act, ig, hq, hd, hi, ho, hv, o_act, o_ig, o_g1, o_b1, o_qkv, o_qkvb, o_d, o_g2, o_b2, o_in, o_inb, o_out, o_last, held, gq, gd, gi, go, gv, arrive, leave
):
    z = lax.axis_index("shard") % 4
    pieces = [(act.at[m], o_act.at[0, m]) for m in (0, 1)] + [(ig.at[m], o_ig.at[0, m]) for m in (0, 1)]
    coming = [pltpu.make_async_copy(src, held.at[k], arrive.at[k]) for k, (src, _) in enumerate(pieces)]
    going = [pltpu.make_async_copy(held.at[k], dst, leave.at[k]) for k, (_, dst) in enumerate(pieces)]
    small = [
        pltpu.make_async_copy(src, dst, arrive.at[4 + k])
        for k, (src, dst) in enumerate(((hq, gq), (hd, gd), (hi, gi), (ho, go), (hv, gv)))
    ]
    for copy in coming + small:
        copy.start()
    for copy, after in zip(coming, going):
        copy.wait()
        after.start()
    for copy in small:
        copy.wait()
    for half in (0, 1):
        rows = slice(16 * half, 16 * half + 16)
        for hp in range(PAIRS):
            for which in range(3):
                column = 512 * which + 128 * hp
                o_qkv[0, rows, column : column + 128] = gq[hp, half, :, 128 * which : 128 * which + 128]
        o_d[0, rows, :] = gd[half]
        o_in[0, rows, :] = gi[half]
        o_out[0, 64 * half : 64 * half + 64, :] = go[half]

    def own(row, width):
        total = jnp.zeros((1, width), F32)
        for k in range(4):
            total = total + jnp.where(z == k, row[:, width * k : width * k + width], 0.0)
        return total

    for row, ref in enumerate((o_g1, o_b1, o_g2, o_b2, o_last)):
        ref[...] = own(gv[row : row + 1, :], 32)
    o_qkvb[...] = own(jnp.concatenate([gv[8 + k : 9 + k, :] for k in range(3)], axis=1), 96)
    o_inb[...] = gv[11:12, :]
    for copy in going:
        copy.wait()


def solution(mesh):
    rows = P(None, ("replica", "shard"), None)
    vector, matrix = P("section", "shard"), P("section", "shard", None)
    slabs = P("section", None, ("replica", "shard"), None)
    return jax.shard_map(
        body,
        mesh=mesh,
        in_specs=(
            rows, rows, rows, vector, vector, matrix, vector, matrix, vector, vector, matrix, vector, matrix, vector,
        ),
        out_specs=(
            slabs, slabs, vector, vector, matrix, vector, matrix, vector, vector, matrix, vector, matrix, vector,
        ),
        check_vma=False,
    )
```

profile of v0, /device:TPU:0, one launch (start us, length us, event | category | flops | bytes accessed | tf_op | source)
XLA Modules:
  0.0 135.1 jit_solution(4421923684108189759)
XLA Ops:
  0.7 130.5 %layers.1 = (bf16[2,768,512]{2,1,0:T(8,128)(2,1)}, bf16[2,768,512]{2,1,0:T(8,128)(2,1)}, f32[4,2,16,384]{3,2,1,0:T(8,128)}, f32[2,16,512]{2,1,0:T(8,128)}, f32[2...) custom-call(s32[2,1,4]{2,1,0:T(1,128)} %lengths.1, ...), custom_call_target="tpu_custom_call" | custom-call | tf_op jit(solution)/shard_map/layers/pallas_call | solution.py:1073
  131.1 3.8 %hand_out.1 = (bf16[1,2,768,512]{3,2,1,0:T(8,128)(2,1)}, bf16[1,2,768,512]{3,2,1,0:T(8,128)(2,1)}, f32[1,32]{1,0:T(1,128)}, f32[1,32]{1,0:T(1,128)}, f32[1,32,15...) custom-call(bf16[2,768,512]{2,1,0:T(8,128)(2,1)} %get-tuple-element., ...), custom_call_target="tpu_custom_call" | custom-call | tf_op jit(solution)/shard_map/hand_out/pallas_call | solution.py:1103
where the time goes:
time: 135 us
  Pallas kernels  134 us (99%)
    pallas_call x1, Pallas kernels, body(): pl.pallas_call(kernel, out_shape=[shape((2, T, D), BF), shape((2, T, D),...  130 us
    pallas_call x1, Pallas kernels, body(): pl.pallas_call(hand_out, out_shape=[slab, slab, vector, vector, shape((1,...  3.8 us

commit v1 on v0

--- a/solution.py
+++ b/solution.py
@@ -445,6 +445,8 @@
     st_rinv,
     st_act,
     st_slo,
+    st_n1t,
+    st_n2,
     *scratch,
 ):
     scratch = list(scratch)
@@ -702,6 +704,7 @@
         (bt, st_bt, 6),
         (rinv, st_rinv, 7),
     ]
+    norms_kept = [(n1t, st_n1t, 12), (n2, st_n2, 13)]
     wide_kept = [(act, st_act, 8), (slo, st_slo, 9)]
 
     fetch("0V2", "0a2", "0b2", "0c2", "0d2")
@@ -711,6 +714,8 @@
     fetch("0V5")
     unpack(0)
     norms(0)
+    for a, b, k in norms_kept:
+        local(a, b, k).start()
     fetch("0b3", "0O2", "0a5")
     fetch("0c3", "0b5")
     loop(2, lambda hp: attend(0, hp))
@@ -736,6 +741,8 @@
     fetch("1V4", "1a4", "1b4")
     fetch("1V5")
     unpack(1)
+    for a, b, k in norms_kept:
+        local(a, b, k).wait()
     norms(1)
     fetch("1c4", "1d4", "1a5", "1b5")
     for a, b, k in attention_kept:
@@ -860,25 +867,27 @@
         weight = jnp.concatenate([group_rows(wq[l].at[hp], t) for hp in range(PAIRS)], axis=1)
         dn1[:, columns(t * 128, 128)] = dg(weight, qkvt[...], 1, 0).astype(BF).T
 
+    def add_sums(u, first, second):
+        dvec[0:1, :] += jnp.sum(first * u, axis=0, keepdims=True)
+        dvec[1:2, :] += jnp.sum(first, axis=0, keepdims=True)
+        dvec[2:3, :] += jnp.sum(second * u, axis=0, keepdims=True)
+        dvec[3:4, :] += jnp.sum(second, axis=0, keepdims=True)
+
     def norm_sums(l):
         def tile(k):
             rows = columns(k * TILE, TILE)
-            u, _ = normed(l, rows)
-            first = dn1[rows, :].astype(F32)
-            second = acc[rows, :]
-            dvec[0:1, :] += jnp.sum(first * u, axis=0, keepdims=True)
-            dvec[1:2, :] += jnp.sum(first, axis=0, keepdims=True)
-            dvec[2:3, :] += jnp.sum(second * u, axis=0, keepdims=True)
-            dvec[3:4, :] += jnp.sum(second, axis=0, keepdims=True)
+            add_sums(normed(l, rows)[0], dn1[rows, :].astype(F32), acc[rows, :])
 
         loop(3, tile)
 
-    def end_back(l):
+    def end_back(l, with_sums):
         def tile(k):
             rows = columns(k * TILE, TILE)
             u, scale = normed(l, rows)
             first = dn1[rows, :].astype(F32)
             second = acc[rows, :]
+            if with_sums:
+                add_sums(u, first, second)
             total = first * vd[0:1, :] + second * vd[2:3, :]
             centre = jnp.mean(total, axis=1, keepdims=True)
             along = jnp.mean(total * u, axis=1, keepdims=True)
@@ -887,7 +896,7 @@
 
         loop(3, tile)
 
-    def put_vectors(l):
+    def put_biases():
         sums = dg(jnp.ones((8, T), BF), qkvt[...], 1, 1)
         for x in range(4):
             for k in range(3):
@@ -897,9 +906,13 @@
         for x in range(4):
             rest = jnp.concatenate([vq[3 * x : 3 * x + 3, :], jnp.zeros((5, 128), F32)], axis=0)
             for z in range(4):
-                gvec[x, z, 0:8] = dvec[:, 128 * x : 128 * x + 128]
                 gvec[x, z, 8:16] = rest
                 gvec[x, z, 11:12] = fvec[x : x + 1, 128 * z : 128 * z + 128]
+
+    def put_norms():
+        for x in range(4):
+            for z in range(4):
+                gvec[x, z, 0:8] = dvec[:, 128 * x : 128 * x + 128]
 
     restored = ((qkvt, st_qkv, 2), (p0, st_p0, 3), (p1, st_p1, 4), (p2, st_p2, 5), (bt, st_bt, 6), (rinv, st_rinv, 7))
 
@@ -918,18 +931,19 @@
     back_pairs(1, 0)
     send("1D1", "1a1", "1O2")
     back_pairs(1, 2)
+    local(st_n1t, n1t, 12).start()
     send("1b1", "1c1", "1I2")
     loop(4, lambda t: back_norm_one(1, t))
     send("1d1", "1D2", "1O3")
-    norm_sums(1)
-    put_vectors(1)
+    put_biases()
     for a, b, k in restored:
         local(b, a, k).start()
+    end_back(1, True)
+    put_norms()
     send("1V0", "1a2")
-    end_back(1)
+    local(st_n2, n2, 13).start()
 
     unpack(0)
-    norms(0)
     start_back(0)
     local(st_act, act, 8).wait()
     local(st_slo, slo, 9).wait()
@@ -938,12 +952,14 @@
     send("0O0", "1V1", "1D3", "1c2", "1d2", "1a3")
     loop(4, lambda c: back_wide(0, c))
     send("0O1", "1O4", "1b3")
+    local(st_n2, n2, 13).wait()
     loop(4, lambda c: back_in(0, c))
     send("0I0", "1V2", "1c3", "1d3", "1D4")
     loop(2, lambda t: back_norm_two(0, t))
     send("0I1", "1I4", "1a4", "1b4")
     for a, b, k in restored:
         local(b, a, k).wait()
+    local(st_n1t, n1t, 12).wait()
     back_dense(0)
     send("0D0")
     back_attend(0, 0)
@@ -958,27 +974,28 @@
     back_attend(0, 3)
     back_qkv(3)
     send("0d0", "0c1")
+    put_biases()
     send("0I2", "0D2", "0a2", "0O3")
     loop(2, lambda t: back_norm_one(0, t))
     send("0d1", "0b2")
     loop(2, lambda t: back_norm_one(0, t + 2))
     norm_sums(0)
-    put_vectors(0)
+    put_norms()
     send("0V0")
-    send("0I3", "0c2", "0D3", "0a3", "0O4")
-    send("0d2")
+    send("0I3")
     send("0V1")
-    end_back(0)
+    send("0c2", "0d2")
+    end_back(0, False)
     grad_mine = local(grad.at[s], ig_out.at[s], 11)
     grad_theirs = remote(grad.at[1 - s], ig_out.at[s], ex_send.at[1], ex_recv.at[1], me.sibling())
     grad_mine.start()
     grad_theirs.start()
-    send("0b3", "0c3", "0d3")
-    send("0D4", "0a4")
+    send("0D3", "0a3", "0b3", "0O4")
+    send("0c3", "0d3")
     send("0V2")
-    send("0b4", "0c4")
-    send("0d4")
+    send("0D4", "0a4", "0b4")
     send("0I4")
+    send("0c4", "0d4")
     send("0V3")
     for l in (1, 0):
         for c in range(PARTS):
@@ -1015,7 +1032,7 @@
         pltpu.VMEM((T, D), F32),
         pltpu.VMEM((T, D), BF),
     ]
-    shapes += [pltpu.VMEM(shape, kind) for shape, kind in KEPT]
+    shapes += [pltpu.VMEM(shape, kind) for shape, kind in KEPT[:8]]
     shapes += [
         pltpu.VMEM((2, TILE, 768), BF),
         pltpu.VMEM((2, TILE, 512), BF),
@@ -1035,7 +1052,7 @@
     ]
     dma = pltpu.SemaphoreType.DMA
     shapes += [dma((2, PARTS, 5))] * 3
-    shapes += [dma((PARTS,)), dma((12,)), dma((2,)), dma((2,))]
+    shapes += [dma((PARTS,)), dma((14,)), dma((2,)), dma((2,))]
     return shapes
 
 
@@ -1048,6 +1065,8 @@
     ((HEADS, T), F32),
     ((T, FF), BF),
     ((T, FF), BF),
+    ((D, T), BF),
+    ((T, D), BF),
 )
 
 

time: 135 us -> 133 us (0.985)
  Pallas kernels: 134 us -> 132 us
    pallas_call x1, Pallas kernels: 130 us -> 128 us  [body(): pl.pallas_call(kernel, out_shape=[shape((2, T, D), BF), shape((2, T, D),...]
where the time goes in v1:
time: 133 us
  Pallas kernels  132 us (99%)
    pallas_call x1, Pallas kernels, body(): pl.pallas_call(kernel, out_shape=[shape((2, T, D), BF), shape((2, T, D),...  128 us
    pallas_call x1, Pallas kernels, body(): pl.pallas_call(hand_out, out_shape=[slab, slab, vector, vector, shape((1,...  3.8 us

profile of v1, /device:TPU:0, one launch (start us, length us, event | category | flops | bytes accessed | tf_op | source)
XLA Modules:
  0.0 132.8 jit_solution(6731962474489451137)
XLA Ops:
  0.7 128.2 %layers.1 = (bf16[2,768,512]{2,1,0:T(8,128)(2,1)}, bf16[2,768,512]{2,1,0:T(8,128)(2,1)}, f32[4,2,16,384]{3,2,1,0:T(8,128)}, f32[2,16,512]{2,1,0:T(8,128)}, f32[2...) custom-call(s32[2,1,4]{2,1,0:T(1,128)} %lengths.1, ...), custom_call_target="tpu_custom_call" | custom-call | tf_op jit(solution)/shard_map/layers/pallas_call | solution.py:1092
  128.8 3.8 %hand_out.1 = (bf16[1,2,768,512]{3,2,1,0:T(8,128)(2,1)}, bf16[1,2,768,512]{3,2,1,0:T(8,128)(2,1)}, f32[1,32]{1,0:T(1,128)}, f32[1,32]{1,0:T(1,128)}, f32[1,32,15...) custom-call(bf16[2,768,512]{2,1,0:T(8,128)(2,1)} %get-tuple-element., ...), custom_call_target="tpu_custom_call" | custom-call | tf_op jit(solution)/shard_map/hand_out/pallas_call | solution.py:1122

commit v2 on v1

--- a/solution.py
+++ b/solution.py
@@ -982,9 +982,9 @@
     norm_sums(0)
     put_norms()
     send("0V0")
+    send("0c2", "0d2")
+    send("0V1")
     send("0I3")
-    send("0V1")
-    send("0c2", "0d2")
     end_back(0, False)
     grad_mine = local(grad.at[s], ig_out.at[s], 11)
     grad_theirs = remote(grad.at[1 - s], ig_out.at[s], ex_send.at[1], ex_recv.at[1], me.sibling())
@@ -994,8 +994,8 @@
     send("0c3", "0d3")
     send("0V2")
     send("0D4", "0a4", "0b4")
+    send("0c4", "0d4")
     send("0I4")
-    send("0c4", "0d4")
     send("0V3")
     for l in (1, 0):
         for c in range(PARTS):

time: 133 us -> 135 us (1.015)
    pallas_call x1, Pallas kernels: 128 us -> 130 us  [body(): pl.pallas_call(kernel, out_shape=[shape((2, T, D), BF), shape((2, T, D),...]
where the time goes in v2:
time: 135 us; the launch traced here: 134 us
  Pallas kernels  133 us (99%)
    pallas_call x1, Pallas kernels, body(): pl.pallas_call(kernel, out_shape=[shape((2, T, D), BF), shape((2, T, D),...  130 us
    pallas_call x1, Pallas kernels, body(): pl.pallas_call(hand_out, out_shape=[slab, slab, vector, vector, shape((1,...  3.8 us

profile of v2, /device:TPU:0, one launch (start us, length us, event | category | flops | bytes accessed | tf_op | source)
XLA Modules:
  0.0 134.3 jit_solution(16933397853722016083)
XLA Ops:
  0.7 129.6 %layers.1 = (bf16[2,768,512]{2,1,0:T(8,128)(2,1)}, bf16[2,768,512]{2,1,0:T(8,128)(2,1)}, f32[4,2,16,384]{3,2,1,0:T(8,128)}, f32[2,16,512]{2,1,0:T(8,128)}, f32[2...) custom-call(s32[2,1,4]{2,1,0:T(1,128)} %lengths.1, ...), custom_call_target="tpu_custom_call" | custom-call | tf_op jit(solution)/shard_map/layers/pallas_call | solution.py:1092
  130.3 3.8 %hand_out.1 = (bf16[1,2,768,512]{3,2,1,0:T(8,128)(2,1)}, bf16[1,2,768,512]{3,2,1,0:T(8,128)(2,1)}, f32[1,32]{1,0:T(1,128)}, f32[1,32]{1,0:T(1,128)}, f32[1,32,15...) custom-call(bf16[2,768,512]{2,1,0:T(8,128)(2,1)} %get-tuple-element., ...), custom_call_target="tpu_custom_call" | custom-call | tf_op jit(solution)/shard_map/hand_out/pallas_call | solution.py:1122
